TPU v7x, 512 devices: a whole 4x4x16 slice. The times are simulated.
512 devices in a mesh: ctx: 32 (over z, y_hi), tp: 8 (over x, y_lo), pool: 2 (over core).
Axes of the slice: x: 4, y: 4 (y_hi: 2, y_lo: 2; y = y_hi * 2 + y_lo), z: 16, core: 2. Of those that a mesh axis runs over, the one named last changes fastest.
Arguments:
- prompt_query: bfloat16 [2, 2, 4096, 8192], P('pool', None, 'ctx', 'tp'), may hold values from -32 to 32
- prompt_kv: bfloat16 [2, 2, 2, 4096, 1024], P('pool', None, None, 'ctx', 'tp'), may hold values from -12 to 12
- block_order: int32 [2, 2, 32], P('pool'), may hold values from 0 to 31, each once within a row
- decode_query: bfloat16 [2, 256, 2, 8192], P('pool', 'ctx', None, 'tp'), may hold values from -32 to 32
- history_kv: bfloat16 [2, 2, 256, 64, 1024], P('pool', None, 'ctx', None, 'tp'), may hold values from -5.5 to 5.5
- new_kv: bfloat16 [2, 2, 256, 2, 1024], P('pool', None, 'ctx', None, 'tp'), may hold values from -7 to 7
- hist_len: int32 [2, 256], P('pool', 'ctx'), may hold values from 1 to 64, as said below
- row_prompt: int32 [2, 256], P('pool', 'ctx'), may hold values from 0 to 1
Outputs:
- prefill_out: bfloat16 [2, 2, 4096, 8192], P('pool', None, ('ctx', 'tp'))
- decode_out: bfloat16 [2, 256, 2, 8192], P('pool', 'ctx', None, 'tp')
Inputs may be any that keep to these rules, and one draw needn't show every extreme that they name: `block_order`: for each group and prompt every block index appears once. `hist_len`: every group has a row of length 64.
All inputs are finite; a program needn't handle non-finite values.
Results may differ from a plain program's by a relative error of at most 0.009.
Values may be sent and summed in bfloat16 or wider, within the bound.
A program may use at most 64 MiB of HBM per device.

v0:
```python
import jax
import jax.numpy as jnp
from jax import lax
from jax.sharding import PartitionSpec as P

QUERY_HEADS = 64
KEY_VALUE_HEADS = 8
HEAD_SIZE = 128


NEG = -1e30


def from_partner(value, axis, bit):
    mask = 2**bit
    pairs = [(source, source ^ mask) for source in range(lax.axis_size(axis))]
    return lax.ppermute(value, axis, pairs)


def block_positions(order_table, row_ids, block_rows):
    owner_block = row_ids // block_rows
    block_count = order_table.shape[1]
    matches = owner_block[None, :, None] == jnp.arange(block_count, dtype=jnp.int32)[None, None, :]
    first_place = jnp.sum(jnp.where(matches, order_table[:, None, :], 0), axis=-1)
    return first_place * block_rows + (row_ids % block_rows)[None, :]


def make_fold(query_rows, query_pos, order_table, block_rows, kv_heads):
    scaling = HEAD_SIZE ** (-0.5)
    prompts = query_rows.shape[0]

    def accumulate(running, incoming, offset):
        key_count = incoming.shape[3]
        step_spacing = 512
        heads_of_keys = incoming[0, 0].reshape(prompts, key_count, kv_heads, HEAD_SIZE)
        heads_of_values = incoming[0, 1].reshape(prompts, key_count, kv_heads, HEAD_SIZE)

        def one_block(block_index, carried):
            weighted, weight_sum, highest = carried
            rows_of_keys = lax.dynamic_slice_in_dim(
                heads_of_keys, block_index * step_spacing, step_spacing, 1
            )
            rows_of_values = lax.dynamic_slice_in_dim(
                heads_of_values, block_index * step_spacing, step_spacing, 1
            )
            row_ids = block_index * step_spacing + jnp.arange(step_spacing, dtype=jnp.int32)
            key_pos = block_positions(order_table, row_ids, block_rows)
            visible = (key_pos[:, None, :] <= query_pos[:, :, None])[:, :, None, None, :]
            scores = (
                jnp.einsum(
                    "pnegd,pmed->pnegm",
                    query_rows,
                    rows_of_keys,
                    preferred_element_type=jnp.float32,
                )
                * scaling
            )
            updated = jnp.maximum(highest, jnp.max(jnp.where(visible, scores, NEG), axis=-1))
            weights = jnp.where(visible, jnp.exp(scores - updated[..., None]), 0.0)
            factor = jnp.exp(highest - updated)
            weight_sum = weight_sum * factor + jnp.sum(weights, axis=-1)
            weighted = weighted * factor[..., None] + jnp.einsum(
                "pnegm,pmed->pnegd",
                weights.astype(jnp.bfloat16),
                rows_of_values,
                preferred_element_type=jnp.float32,
            )
            return (weighted, weight_sum, updated)

        return lax.fori_loop(0, key_count // step_spacing, one_block, running)

    return accumulate


def own_parts(decode_heads, history_kv, new_kv, hist_len, kv_heads):
    scaling = HEAD_SIZE ** (-0.5)
    row_count, step_count = (decode_heads.shape[0], decode_heads.shape[1])
    history_span = history_kv.shape[3]
    history_keys = history_kv[0, 0].reshape(row_count, history_span, kv_heads, HEAD_SIZE)
    history_values = history_kv[0, 1].reshape(row_count, history_span, kv_heads, HEAD_SIZE)
    fresh_keys = new_kv[0, 0].reshape(row_count, step_count, kv_heads, HEAD_SIZE)
    fresh_values = new_kv[0, 1].reshape(row_count, step_count, kv_heads, HEAD_SIZE)
    hist_scores = (
        jnp.einsum(
            "rsegd,rjed->rsegj", decode_heads, history_keys, preferred_element_type=jnp.float32
        )
        * scaling
    )
    hist_visible = (jnp.arange(history_span, dtype=jnp.int32)[None, :] < hist_len[0][:, None])[
        :, None, None, None, :
    ]
    new_scores = (
        jnp.einsum(
            "rsegd,rjed->rsegj", decode_heads, fresh_keys, preferred_element_type=jnp.float32
        )
        * scaling
    )
    new_visible = (
        jnp.arange(step_count, dtype=jnp.int32)[None, :]
        <= jnp.arange(step_count, dtype=jnp.int32)[:, None]
    )[None, :, None, None, :]
    return ((hist_scores, hist_visible, history_values), (new_scores, new_visible, fresh_values))


def own_highest(own_keys):
    first_part, second_part = own_keys
    return jnp.maximum(
        jnp.max(jnp.where(first_part[1], first_part[0], NEG), axis=-1),
        jnp.max(jnp.where(second_part[1], second_part[0], NEG), axis=-1),
    )


def own_terms(own_keys, highest):
    weighted = 0.0
    weight_sum = 0.0
    for scores, visible, values in own_keys:
        weights = jnp.where(visible, jnp.exp(scores - highest[..., None]), 0.0)
        weight_sum = weight_sum + jnp.sum(weights, axis=-1)
        weighted = weighted + jnp.einsum(
            "rsegj,rjed->rsegd",
            weights.astype(jnp.bfloat16),
            values,
            preferred_element_type=jnp.float32,
        )
    return (weighted, weight_sum)


def prompt_scores(decode_heads, rows_of_keys):
    return jnp.einsum(
        "rsegd,pled->rsegpl", decode_heads, rows_of_keys, preferred_element_type=jnp.float32
    ) * HEAD_SIZE ** (-0.5)


def decode_cached(decode_heads, handed, row_prompt, own_keys, kv_heads):
    prompts, span_rows = (handed.shape[2], handed.shape[3])
    rows_of_keys = handed[0, 0].reshape(prompts, span_rows, kv_heads, HEAD_SIZE)
    rows_of_values = handed[0, 1].reshape(prompts, span_rows, kv_heads, HEAD_SIZE)
    scores = prompt_scores(decode_heads, rows_of_keys)
    visible = (row_prompt[0][:, None] == jnp.arange(prompts, dtype=jnp.int32)[None, :])[
        :, None, None, None, :, None
    ]
    highest = jnp.maximum(
        jnp.max(jnp.where(visible, scores, NEG), axis=(-2, -1)), own_highest(own_keys)
    )
    weights = jnp.where(visible, jnp.exp(scores - highest[..., None, None]), 0.0)
    weighted = jnp.einsum(
        "rsegpl,pled->rsegd",
        weights.astype(jnp.bfloat16),
        rows_of_values,
        preferred_element_type=jnp.float32,
    )
    extra, extra_sum = own_terms(own_keys, highest)
    return (weighted + extra) / (jnp.sum(weights, axis=(-2, -1)) + extra_sum)[..., None]


def per_device(
    prompt_query, prompt_kv, block_order, decode_query, history_kv, new_kv, hist_len, row_prompt
):
    kv_heads = prompt_kv.shape[-1] // HEAD_SIZE
    group_width = QUERY_HEADS // KEY_VALUE_HEADS
    prompts, block_rows = (prompt_query.shape[1], prompt_query.shape[2])
    query_rows = prompt_query[0].reshape(prompts, block_rows, kv_heads, group_width, HEAD_SIZE)
    order_table = block_order[0]
    row_ids = lax.axis_index("ctx") * block_rows + jnp.arange(block_rows, dtype=jnp.int32)
    query_pos = block_positions(order_table, row_ids, block_rows)
    accumulate = make_fold(query_rows, query_pos, order_table, block_rows, kv_heads)
    head_shape = (prompts, block_rows, kv_heads, group_width)
    initial = (
        jnp.zeros(head_shape + (HEAD_SIZE,), jnp.float32),
        jnp.zeros(head_shape, jnp.float32),
        jnp.full(head_shape, NEG, jnp.float32),
    )
    running = accumulate(
        initial, lax.all_gather(prompt_kv, "ctx", axis=3, tiled=True), jnp.int32(0)
    )
    weighted, weight_sum, highest = running
    local_out = (
        (weighted / weight_sum[..., None])
        .astype(jnp.bfloat16)
        .reshape(1, prompts, block_rows, kv_heads * group_width * HEAD_SIZE)
    )
    prefill_out = lax.all_to_all(local_out, "tp", split_axis=2, concat_axis=3, tiled=True)
    row_count, step_count = (decode_query.shape[1], decode_query.shape[2])
    decode_heads = decode_query[0].reshape(row_count, step_count, kv_heads, group_width, HEAD_SIZE)
    own_keys = own_parts(decode_heads, history_kv, new_kv, hist_len, kv_heads)
    prompt_block = from_partner(prompt_kv, "pool", 0)
    handed = lax.all_gather(prompt_block, "ctx", axis=3, tiled=True)
    attended = decode_cached(decode_heads, handed, row_prompt, own_keys, kv_heads)
    decode_out = attended.astype(jnp.bfloat16).reshape(
        1, row_count, step_count, kv_heads * group_width * HEAD_SIZE
    )
    return (prefill_out, decode_out)


def solution(mesh):
    placed = (
        P("pool", None, "ctx", "tp"),
        P("pool", None, None, "ctx", "tp"),
        P("pool", None, None),
        P("pool", "ctx", None, "tp"),
        P("pool", None, "ctx", None, "tp"),
        P("pool", None, "ctx", None, "tp"),
        P("pool", "ctx"),
        P("pool", "ctx"),
    )
    return jax.shard_map(
        per_device,
        mesh=mesh,
        in_specs=placed,
        out_specs=(P("pool", None, ("ctx", "tp"), None), P("pool", "ctx", None, "tp")),
        check_vma=False,
    )
```

profile of v0, /device:TPU:6, one launch (start us, length us, event | category | flops | bytes accessed | tf_op | source)
XLA Modules:
  0.0 355.9 jit_solution(14845162501648736327)
XLA Ops:
  7.9 1.9 collective-permute-start
  12.9 1.0 select_reduce_fusion.4
  14.7 1.3 copy.37
  16.3 1.2 select_reduce_fusion.2
  18.1 161.5 %all-gather.3.cloned.1.call-done = bf16[1,2,2,4096,128]{4,3,2,1,0:T(8,128)(2,1)} async-done(((bf16[1,2,2,128,128]{4,3,2,1,0:T(8,128)(2,1)}), bf16[1,2,2,4096,128]{4,3,2,1,0:T(8,128)(2,1)}) %all-gather.3.cloned.1.call-update) | async-done | bytes 4194320 | tf_op jit(solution)/shard_map/all_gather | solution.py:174
  179.6 3.9 %slice_bitcast_fusion.4 = (bf16[2,4096,1,128]{3,1,0,2:T(8,128)(2,1)}, bf16[2,4096,1,128]{3,1,0,2:T(8,128)(2,1)S(1)}) fusion(bf16[1,2,2,4096,128]{4,3,2,1,0:T(8,128)(2,1)} %all-gather.3.cloned.1.call-done), kind=kLoop, calls=%fused_computation.55 | loop fusion | bytes 8388608 | tf_op jit(solution)/shard_map/reshape;squeeze | solution.py:36
  183.5 69.2 %while.20 = (s32[]{:T(128)}, f32[2,128,1,8,128]{1,4,3,0,2:T(8,128)}, f32[2,128,1,8]{1,3,0,2:T(8,128)S(1)}, f32[2,128,1,8]{1,3,0,2:T(8,128)S(1)}, s32[1,2,32]{2,1...) while((s32[]{:T(128)}, ...), condition=%wide.region_5.6_spmd.clone, body=%wide.region_1.5_spmd.clone.sunk | while | flops 549428224 | bytes 33220068 | solution.py:70
  183.9 2.7 fusion.75
  186.6 4.4 %fusion.77 = f32[2,128,1,8,128]{1,4,3,0,2:T(8,128)} fusion(f32[2,512,128,8]{2,1,3,0:T(8,128)} %get-tuple-element.395, f32[2,128,8]{1,2,0:T(8,128)S(1)} %bitcast.208, pred[2,128,512]{1,2,0:T(8,128)(4,1)S(1)} %broadcast_compare_fusion.2, f32[2,128,1,8,128]{1,4,3,0,2:T(8,128)} %get-tuple-element.413, f32[2,128,8]{1,2,0:T(8,128)S(1)} %get-tuple-element.398, ...), kind=kOutput, calls=%fused_computation.14.clone.1 | convolution fusion | flops 273416192 | bytes 6701061 | tf_op jit(solution)/shard_map/while/body/eval_jaxpr/pnegm,pmed->pnegd/dot_general | solution.py:62
  191.0 0.9 fusion.78
  192.3 2.7 fusion.75
  195.0 4.7 %fusion.77 = f32[2,128,1,8,128]{1,4,3,0,2:T(8,128)} fusion(f32[2,512,128,8]{2,1,3,0:T(8,128)} %get-tuple-element.395, f32[2,128,8]{1,2,0:T(8,128)S(1)} %bitcast.208, pred[2,128,512]{1,2,0:T(8,128)(4,1)S(1)} %broadcast_compare_fusion.2, f32[2,128,1,8,128]{1,4,3,0,2:T(8,128)} %get-tuple-element.413, f32[2,128,8]{1,2,0:T(8,128)S(1)} %get-tuple-element.398, ...), kind=kOutput, calls=%fused_computation.14.clone.1 | convolution fusion | flops 273416192 | bytes 6701061 | tf_op jit(solution)/shard_map/while/body/eval_jaxpr/pnegm,pmed->pnegd/dot_general | solution.py:62
  199.7 0.9 fusion.78
  201.0 2.7 fusion.75
  203.7 4.7 %fusion.77 = f32[2,128,1,8,128]{1,4,3,0,2:T(8,128)} fusion(f32[2,512,128,8]{2,1,3,0:T(8,128)} %get-tuple-element.395, f32[2,128,8]{1,2,0:T(8,128)S(1)} %bitcast.208, pred[2,128,512]{1,2,0:T(8,128)(4,1)S(1)} %broadcast_compare_fusion.2, f32[2,128,1,8,128]{1,4,3,0,2:T(8,128)} %get-tuple-element.413, f32[2,128,8]{1,2,0:T(8,128)S(1)} %get-tuple-element.398, ...), kind=kOutput, calls=%fused_computation.14.clone.1 | convolution fusion | flops 273416192 | bytes 6701061 | tf_op jit(solution)/shard_map/while/body/eval_jaxpr/pnegm,pmed->pnegd/dot_general | solution.py:62
  209.7 2.7 fusion.75
  212.4 4.7 %fusion.77 = f32[2,128,1,8,128]{1,4,3,0,2:T(8,128)} fusion(f32[2,512,128,8]{2,1,3,0:T(8,128)} %get-tuple-element.395, f32[2,128,8]{1,2,0:T(8,128)S(1)} %bitcast.208, pred[2,128,512]{1,2,0:T(8,128)(4,1)S(1)} %broadcast_compare_fusion.2, f32[2,128,1,8,128]{1,4,3,0,2:T(8,128)} %get-tuple-element.413, f32[2,128,8]{1,2,0:T(8,128)S(1)} %get-tuple-element.398, ...), kind=kOutput, calls=%fused_computation.14.clone.1 | convolution fusion | flops 273416192 | bytes 6701061 | tf_op jit(solution)/shard_map/while/body/eval_jaxpr/pnegm,pmed->pnegd/dot_general | solution.py:62
  218.3 2.7 fusion.75
  221.1 4.7 %fusion.77 = f32[2,128,1,8,128]{1,4,3,0,2:T(8,128)} fusion(f32[2,512,128,8]{2,1,3,0:T(8,128)} %get-tuple-element.395, f32[2,128,8]{1,2,0:T(8,128)S(1)} %bitcast.208, pred[2,128,512]{1,2,0:T(8,128)(4,1)S(1)} %broadcast_compare_fusion.2, f32[2,128,1,8,128]{1,4,3,0,2:T(8,128)} %get-tuple-element.413, f32[2,128,8]{1,2,0:T(8,128)S(1)} %get-tuple-element.398, ...), kind=kOutput, calls=%fused_computation.14.clone.1 | convolution fusion | flops 273416192 | bytes 6701061 | tf_op jit(solution)/shard_map/while/body/eval_jaxpr/pnegm,pmed->pnegd/dot_general | solution.py:62
  227.0 2.7 fusion.75
  229.7 4.7 %fusion.77 = f32[2,128,1,8,128]{1,4,3,0,2:T(8,128)} fusion(f32[2,512,128,8]{2,1,3,0:T(8,128)} %get-tuple-element.395, f32[2,128,8]{1,2,0:T(8,128)S(1)} %bitcast.208, pred[2,128,512]{1,2,0:T(8,128)(4,1)S(1)} %broadcast_compare_fusion.2, f32[2,128,1,8,128]{1,4,3,0,2:T(8,128)} %get-tuple-element.413, f32[2,128,8]{1,2,0:T(8,128)S(1)} %get-tuple-element.398, ...), kind=kOutput, calls=%fused_computation.14.clone.1 | convolution fusion | flops 273416192 | bytes 6701061 | tf_op jit(solution)/shard_map/while/body/eval_jaxpr/pnegm,pmed->pnegd/dot_general | solution.py:62
  235.7 2.7 fusion.75
  238.4 4.7 %fusion.77 = f32[2,128,1,8,128]{1,4,3,0,2:T(8,128)} fusion(f32[2,512,128,8]{2,1,3,0:T(8,128)} %get-tuple-element.395, f32[2,128,8]{1,2,0:T(8,128)S(1)} %bitcast.208, pred[2,128,512]{1,2,0:T(8,128)(4,1)S(1)} %broadcast_compare_fusion.2, f32[2,128,1,8,128]{1,4,3,0,2:T(8,128)} %get-tuple-element.413, f32[2,128,8]{1,2,0:T(8,128)S(1)} %get-tuple-element.398, ...), kind=kOutput, calls=%fused_computation.14.clone.1 | convolution fusion | flops 273416192 | bytes 6701061 | tf_op jit(solution)/shard_map/while/body/eval_jaxpr/pnegm,pmed->pnegd/dot_general | solution.py:62
  244.4 2.7 fusion.75
  247.1 4.7 %fusion.77 = f32[2,128,1,8,128]{1,4,3,0,2:T(8,128)} fusion(f32[2,512,128,8]{2,1,3,0:T(8,128)} %get-tuple-element.395, f32[2,128,8]{1,2,0:T(8,128)S(1)} %bitcast.208, pred[2,128,512]{1,2,0:T(8,128)(4,1)S(1)} %broadcast_compare_fusion.2, f32[2,128,1,8,128]{1,4,3,0,2:T(8,128)} %get-tuple-element.413, f32[2,128,8]{1,2,0:T(8,128)S(1)} %get-tuple-element.398, ...), kind=kOutput, calls=%fused_computation.14.clone.1 | convolution fusion | flops 273416192 | bytes 6701061 | tf_op jit(solution)/shard_map/while/body/eval_jaxpr/pnegm,pmed->pnegd/dot_general | solution.py:62
  252.7 1.3 divide_convert_fusion
  254.1 1.1 copy.61
  255.2 4.8 %all-to-all-start = ((bf16[1,2,128,1024]{3,1,0,2:T(2,128)(2,1)}), bf16[1,2,128,1024]{3,1,0,2:T(2,128)(2,1)S(1)}, u32[]{:S(2)}, u32[]{:S(2)}) async-start(bf16[1,2,128,1024]{3,1,0,2:T(2,128)(2,1)} %copy.61), calls=%async_computation | async-start | bytes 1048576 | tf_op jit(solution)/shard_map/all_to_all | solution.py:182
  260.1 81.5 %all-gather.5.cloned.1.call-done = bf16[1,2,2,4096,128]{4,3,2,1,0:T(8,128)(2,1)} async-done(((bf16[1,2,2,128,128]{4,3,2,1,0:T(8,128)(2,1)}), bf16[1,2,2,4096,128]{4,3,2,1,0:T(8,128)(2,1)}) %all-gather.5.cloned.1.call-update) | async-done | bytes 4194320 | tf_op jit(solution)/shard_map/all_gather | solution.py:187
  341.5 2.4 select_reduce_fusion.1
  345.1 1.0 copy-done.3
  346.1 0.9 fusion.36
  (127 shorter events, 16.8 us)
Async XLA Ops:
  7.2 172.5 %all-gather.3.cloned.1.call-start = ((), (), s32[]{:S(2)}) async-start(), calls=%async_computation.1 | async-start | bytes 4325376 | tf_op jit(solution)/shard_map/all_gather | solution.py:174
  7.9 333.6 %all-gather.5.cloned.1.call-start = ((), (), s32[]{:S(2)}) async-start(), calls=%async_computation.2 | async-start | bytes 4325376 | tf_op jit(solution)/shard_map/all_gather | solution.py:187
  7.9 9.5 %collective-permute-start = (bf16[1,2,2,128,128]{4,3,2,1,0:T(8,128)(2,1)}, bf16[1,2,2,128,128]{4,3,2,1,0:T(8,128)(2,1)S(1)}, u32[]{:S(2)}, u32[]{:S(2)}) collective-permute-start(bf16[1,2,2,128,128]{4,3,2,1,0:T(8,128)(2,1)} %param.11), channel_id=1, source_target_pairs={{0,1},{1,0},{2,3},{3,2},{4,5},{5,4},{6,7},{7,6},{8,9},{9,8},{10,11... | collective-permute-start | bytes 393224 | tf_op jit(solution)/shard_map/ppermute | solution.py:17
  17.5 0.6 copy-start.1
  18.1 165.4 %copy-start.2 = (s32[1,2,32]{2,1,0:T(2,128)S(1)}, s32[1,2,32]{2,1,0:T(2,128)}, u32[]{:S(2)}) copy-start(s32[1,2,32]{2,1,0:T(2,128)} %param.12) | copy-start | bytes 772
  186.6 4.4 %copy-start = (f32[2,512,128,8]{2,1,3,0:T(8,128)S(1)}, f32[2,512,128,8]{2,1,3,0:T(8,128)}, u32[]{:S(2)}) copy-start(f32[2,512,128,8]{2,1,3,0:T(8,128)} %get-tuple-element.395) | copy-start | bytes 12582916 | tf_op jit(solution)/shard_map/while
  195.0 4.7 %copy-start = (f32[2,512,128,8]{2,1,3,0:T(8,128)S(1)}, f32[2,512,128,8]{2,1,3,0:T(8,128)}, u32[]{:S(2)}) copy-start(f32[2,512,128,8]{2,1,3,0:T(8,128)} %get-tuple-element.395) | copy-start | bytes 12582916 | tf_op jit(solution)/shard_map/while
  203.7 4.7 %copy-start = (f32[2,512,128,8]{2,1,3,0:T(8,128)S(1)}, f32[2,512,128,8]{2,1,3,0:T(8,128)}, u32[]{:S(2)}) copy-start(f32[2,512,128,8]{2,1,3,0:T(8,128)} %get-tuple-element.395) | copy-start | bytes 12582916 | tf_op jit(solution)/shard_map/while
  212.4 4.7 %copy-start = (f32[2,512,128,8]{2,1,3,0:T(8,128)S(1)}, f32[2,512,128,8]{2,1,3,0:T(8,128)}, u32[]{:S(2)}) copy-start(f32[2,512,128,8]{2,1,3,0:T(8,128)} %get-tuple-element.395) | copy-start | bytes 12582916 | tf_op jit(solution)/shard_map/while
  221.0 4.7 %copy-start = (f32[2,512,128,8]{2,1,3,0:T(8,128)S(1)}, f32[2,512,128,8]{2,1,3,0:T(8,128)}, u32[]{:S(2)}) copy-start(f32[2,512,128,8]{2,1,3,0:T(8,128)} %get-tuple-element.395) | copy-start | bytes 12582916 | tf_op jit(solution)/shard_map/while
  229.7 4.7 %copy-start = (f32[2,512,128,8]{2,1,3,0:T(8,128)S(1)}, f32[2,512,128,8]{2,1,3,0:T(8,128)}, u32[]{:S(2)}) copy-start(f32[2,512,128,8]{2,1,3,0:T(8,128)} %get-tuple-element.395) | copy-start | bytes 12582916 | tf_op jit(solution)/shard_map/while
  238.4 4.7 %copy-start = (f32[2,512,128,8]{2,1,3,0:T(8,128)S(1)}, f32[2,512,128,8]{2,1,3,0:T(8,128)}, u32[]{:S(2)}) copy-start(f32[2,512,128,8]{2,1,3,0:T(8,128)} %get-tuple-element.395) | copy-start | bytes 12582916 | tf_op jit(solution)/shard_map/while
  247.1 4.7 %copy-start = (f32[2,512,128,8]{2,1,3,0:T(8,128)S(1)}, f32[2,512,128,8]{2,1,3,0:T(8,128)}, u32[]{:S(2)}) copy-start(f32[2,512,128,8]{2,1,3,0:T(8,128)} %get-tuple-element.395) | copy-start | bytes 12582916 | tf_op jit(solution)/shard_map/while
  255.2 92.9 %all-to-all-start = ((bf16[1,2,128,1024]{3,1,0,2:T(2,128)(2,1)}), bf16[1,2,128,1024]{3,1,0,2:T(2,128)(2,1)S(1)}, u32[]{:S(2)}, u32[]{:S(2)}) async-start(bf16[1,2,128,1024]{3,1,0,2:T(2,128)(2,1)} %copy.61), calls=%async_computation | async-start | bytes 1048576 | tf_op jit(solution)/shard_map/all_to_all | solution.py:182
  343.9 2.2 copy-start.3
  344.8 2.2 copy-start.4
  346.1 1.1 copy-start.5
Sparse Core Ops, SparseCore 0:
  11.1 168.4 all-gather.2
  182.8 158.7 all-gather.4
where the time goes:
time: 357 us; the launch traced here: 356 us
  waiting for transfers between devices  244 us (68%)
  matrix products  64.7 us (18%)
  other arithmetic  14.5 us (4%)
  between operations  14.3 us (4%)
  local copies, waits for them, and re-layouts  11.5 us (3%)
  starting transfers between devices  6.83 us (2%)
    all_gather x1, waiting for transfers between devices, per_device(): lax.all_gather(prompt_kv, 'ctx', axis=3, tiled=True)  161 us
    all_gather x1, waiting for transfers between devices, per_device(): handed = lax.all_gather(prompt_block, 'ctx', axis=3, tiled=True)  81.5 us
    dot_general x8, matrix products, one_block(): jnp.einsum('pnegm,pmed->pnegd', weights.astype(jnp.bfloat16), rows_of_val...  37.2 us
    dot_general x8, matrix products, one_block(): jnp.einsum('pnegd,pmed->pnegm', query_rows, rows_of_keys, preferred_eleme...  21.6 us
  transfers between devices with their start and end apart: 4, of which 2 were waited for; matrix products, arithmetic and copies ran while one was open for 25% of the time, Pallas kernels for 0%

commit v1 on v0

v1 whole, which is shorter than its diff:
```python
import functools

import jax
import jax.numpy as jnp
from jax import lax
from jax.experimental import pallas as pl
from jax.experimental.pallas import tpu as pltpu
from jax.sharding import PartitionSpec as P

HEAD_SIZE = 128
NEG = -1e30
SCALE = 1.4426950408889634 / HEAD_SIZE**0.5
NT = (((1,), (1,)), ((), ()))
TN = (((0,), (0,)), ((), ()))
MESH = pl.DeviceIdType.MESH
EARLY = 2
ONES = 16


def kernel(
    half,
    tps,
    order,
    hist_len,
    row_prompt,
    pq,
    pkv,
    dq,
    hist,
    new,
    out,
    dout,
    buf,
    psend,
    q1,
    dqs,
    dqr,
    acc,
    top,
    stage,
    dstage,
    din,
    dloc,
    ring_send,
    ring_recv,
    x_send,
    x_recv,
    q_send,
    q_recv,
    d_send,
    d_recv,
    r_send,
    r_recv,
    o_send,
    o_recv,
    o_local,
):
    ctx, tp, core = lax.axis_index("ctx"), lax.axis_index("tp"), lax.axis_index("pool")
    zs = 2 * half
    z, yh = ctx // 2, ctx % 2
    rows = 128 // tps

    def dev(z_, yh_, tp_, core_):
        return {"ctx": z_ * 2 + yh_, "tp": tp_, "pool": core_}

    right = dev(lax.rem(z + 1, zs), yh, tp, core)
    left = dev(lax.rem(z + zs - 1, zs), yh, tp, core)
    partner = dev(z, 1 - yh, tp, core)
    helpers = (dev(z, yh, tp, 1 - core), dev(z, 1 - yh, tp, 1 - core))

    def other_tp(k):
        return lax.rem(tp + k, tps)

    owners = [[dev(z, yh, other_tp(k), core) for k in range(tps)], [dev(z, 1 - yh, other_tp(k), core) for k in range(tps)]]

    def remote(src, dst, send, recv, device):
        return pltpu.make_async_remote_copy(
            src_ref=src, dst_ref=dst, send_sem=send, recv_sem=recv, device_id=device, device_id_type=MESH
        )

    barrier = pltpu.get_barrier_semaphore()
    peers = [right, left, *helpers, *owners[0][1:], *owners[1]]
    for peer in peers:
        pl.semaphore_signal(barrier, inc=1, device_id=peer, device_id_type=MESH)

    def slab(dst, prompt):
        dst[0:128, :] = pkv[0, 0, prompt]
        dst[128:256, :] = pkv[0, 1, prompt].astype(jnp.float32).T.astype(jnp.bfloat16)

    slab(buf.at[0, 0], yh)
    slab(psend, 1 - yh)
    heads = [dq[:, h * 128 : (h + 1) * 128] for h in range(8)]
    dqt = jnp.concatenate(heads, axis=0)
    dqs[...] = dqt
    pl.semaphore_wait(barrier, len(peers))

    def ring(k, c, src=None):
        return remote(
            buf.at[k - 1, c] if src is None else src,
            buf.at[k, c],
            ring_send.at[k, c],
            ring_recv.at[k, c],
            right if c < 2 else left,
        )

    x_copy = remote(psend, buf.at[0, 1], x_send, x_recv, partner)
    q_copies = [
        remote(pq.at[0, 1 - yh, :, t * 256 : (t + 1) * 256], q1.at[t], q_send.at[t], q_recv.at[t], partner)
        for t in range(4)
    ]
    d_copies = [remote(dqs, dqr.at[i], d_send.at[i], d_recv.at[i], helpers[i]) for i in range(2)]
    x_copy.start()
    ring(1, 0).start()
    ring(1, 2, buf.at[0, 0]).start()
    for copy in d_copies + q_copies:
        copy.start()

    def event(k, c):
        ring(k, c).wait_recv()
        if c in (0, 3):

            @pl.when(k < half)
            def _():
                ring(k + 1, c).start()

        else:

            @pl.when(k + 1 < half)
            def _():
                ring(k + 1, c).start()

    lane = lax.broadcasted_iota(jnp.int32, (1, 128), 1)
    lane_row, lane_step = lax.rem(lane, 16) // 2, lax.rem(lane, 2)
    hs = lax.dot_general(hist[0, 0].reshape(512, 128), dqt, NT, preferred_element_type=jnp.float32) * SCALE
    key_in_row = lax.broadcasted_iota(jnp.int32, (64, 128), 0)
    hs = jnp.concatenate(
        [
            jnp.where((lane_row == r) & (key_in_row < hist_len[0, r]), hs[r * 64 : (r + 1) * 64], NEG)
            for r in range(8)
        ],
        axis=0,
    )
    ns = lax.dot_general(new[0], dqt, NT, preferred_element_type=jnp.float32) * SCALE
    key = lax.broadcasted_iota(jnp.int32, (16, 128), 0)
    ns = jnp.where((key // 2 == lane_row) & (lax.rem(key, 2) <= lane_step), ns, NEG)
    highest = jnp.maximum(jnp.max(hs, axis=0, keepdims=True), jnp.max(ns, axis=0, keepdims=True))
    hw, nw = jnp.exp2(hs - highest), jnp.exp2(ns - highest)
    weighted = lax.dot_general(
        hist[0, 1].reshape(512, 128), hw.astype(jnp.bfloat16), TN, preferred_element_type=jnp.float32
    ) + lax.dot_general(new[1], nw.astype(jnp.bfloat16), TN, preferred_element_type=jnp.float32)
    dloc[0:128] = weighted
    dloc[128:136] = jnp.broadcast_to(jnp.sum(hw, 0, keepdims=True) + jnp.sum(nw, 0, keepdims=True), (8, 128))
    dloc[136:144] = jnp.broadcast_to(highest, (8, 128))

    def queries(t):
        if t == 8:
            return dqr[...].reshape(256, 128)
        x = pq[0, yh, :, t * 256 : (t + 1) * 256] if t < 4 else q1[t - 4]
        return jnp.concatenate([x[:, :128], x[:, 128:]], axis=0)

    causal = lax.rem(lax.broadcasted_iota(jnp.int32, (128, 256), 1), 128) >= lax.broadcasted_iota(
        jnp.int32, (128, 256), 0
    )

    def place(z_, yh_):
        return order[0, yh, lax.rem(z_ + zs, zs) * 2 + yh_]

    own_place = (place(z, yh), place(z, 1 - yh))

    def attend(tiles, u, chunks, sources, first=False):
        keys = jnp.concatenate([buf[u, c, 0:128, :] for c in chunks], axis=0)
        values = jnp.concatenate(
            [
                jnp.concatenate([buf[u, c, 128:256, :] for c in chunks], axis=1),
                jnp.ones((ONES, 128 * len(chunks)), jnp.bfloat16),
            ],
            axis=0,
        )
        places = [place(*s) for s in sources]
        bias = [[jnp.where(pk <= own_place[i], 0.0, NEG).astype(jnp.float32) for pk in places] for i in range(2)]

        def scores(t):
            return lax.dot_general(keys, queries(t), NT, preferred_element_type=jnp.float32)

        def weights(t, s):
            s = s * SCALE
            parts = [s[i * 128 : (i + 1) * 128] for i in range(len(chunks))]
            shift = [None] * len(chunks)
            if t < 8:
                shift = list(bias[t // 4])
                if first:
                    shift[t // 4] = None
                    parts[t // 4] = jnp.where(causal, parts[t // 4], NEG)
            tops = [jnp.max(x, axis=0, keepdims=True) for x in parts]
            tops = [x if b is None else x + b for x, b in zip(tops, shift)]
            now = functools.reduce(jnp.maximum, tops)
            factor = None
            if not first:
                before = top[t, 0:1]
                now = jnp.maximum(now, before)
                factor = jnp.exp2(before - now)
            top[t, 0:1] = now
            w = [jnp.exp2(x - (now if b is None else now - b)).astype(jnp.bfloat16) for x, b in zip(parts, shift)]
            return jnp.concatenate(w, axis=0), factor

        def add(t, w, factor):
            o = jnp.dot(values, w, preferred_element_type=jnp.float32)
            acc[t] = o if factor is None else acc[t] * factor + o

        s = {i: scores(tiles[i]) for i in range(min(2, len(tiles)))}
        w = {0: weights(tiles[0], s[0])}
        for i in range(len(tiles)):
            if i + 2 < len(tiles):
                s[i + 2] = scores(tiles[i + 2])
            if i + 1 < len(tiles):
                w[i + 1] = weights(tiles[i + 1], s[i + 1])
            add(tiles[i], *w[i])

    def step_sources(k):
        return [(z - k, yh), (z - k, 1 - yh), (z + k, yh), (z + k, 1 - yh)]

    def own(tiles):
        attend(tiles, 0, (0, 1), [(z, yh), (z, 1 - yh)], first=True)

    def step(k, tiles):
        attend(tiles, k, (0, 1, 2, 3), step_sources(k))

    x_copy.wait_recv()
    ring(1, 1).start()
    ring(1, 3, buf.at[0, 1]).start()
    own([0, 1, 2, 3])
    event(1, 0)
    event(1, 2)
    for copy in d_copies:
        copy.wait_recv()
    own([8])
    event(1, 1)
    event(1, 3)

    early = min(EARLY, half - 2)

    def early_step(k, _):
        step(k, [0, 1, 2])
        event(k + 1, 0)
        event(k + 1, 2)
        step(k, [3, 8])
        event(k + 1, 1)
        event(k + 1, 3)
        return 0

    lax.fori_loop(1, early + 1, early_step, 0)
    for copy in q_copies:
        copy.wait_recv()
    own([4, 5, 6, 7])

    def middle_step(k, _):
        step(k, [0, 1, 2, 3, 4, 5, 6])
        event(k + 1, 0)
        event(k + 1, 2)
        step(k, [7, 8])
        step(k - early, [4, 5, 6, 7])
        event(k + 1, 1)
        event(k + 1, 3)
        return 0

    middle_end = min(2 * early + 1, half - 1)
    lax.fori_loop(early + 1, middle_end, middle_step, 0)

    def late_step(k, _):
        step(k, [8, 4, 5, 6])
        event(k + 1, 0)

        @pl.when(k + 1 < half)
        def _():
            event(k + 1, 2)

        step(k, [7, 0, 1, 2, 3])

        @pl.when(k + 1 < half)
        def _():
            event(k + 1, 1)

        event(k + 1, 3)
        return 0

    for u in range(middle_end - early, early + 1):
        step(u, [4, 5, 6, 7])
    lax.fori_loop(middle_end, half, late_step, 0)

    far = [(z - half, yh), (z + half, 1 - yh)]
    attend([8, 4, 5, 6, 7, 0, 1, 2, 3], half, (0, 3), far)
    r_copies = []
    for i in range(2):
        dstage[i, 0:136] = acc[8, 0:136, i * 128 : (i + 1) * 128]
        dstage[i, 136:144] = jnp.broadcast_to(top[8, 0:1, i * 128 : (i + 1) * 128], (8, 128))
        r_copies.append(remote(dstage.at[i], din.at[yh], r_send.at[i], r_recv.at[i], helpers[i]))
        r_copies[i].start()

    o_copies = []
    for item in (1, 0):
        for t in range(4):
            a = acc[item * 4 + t]
            o = a[0:128] / a[128:129]
            for h in range(2):
                col = (2 * t + h) * 128
                stage[item, :, col : col + 128] = o[:, h * 128 : (h + 1) * 128].T.astype(jnp.bfloat16)
        for k in range(tps):
            src = stage.at[item, pl.ds(pl.multiple_of(other_tp(k) * rows, rows), rows), :]
            dst = out.at[0, yh, :, pl.ds(pl.multiple_of(tp * 1024, 1024), 1024)]
            if item == 0 and k == 0:
                local = pltpu.make_async_copy(src, dst, o_local)
                local.start()
            else:
                o_copies.append(remote(src, dst, o_send.at[item, k], o_recv.at[item, k], owners[item][k]))
                o_copies[-1].start()

    for copy in r_copies:
        copy.wait_recv()
    wanted = jnp.zeros((1, 128), jnp.int32)
    for r in range(8):
        wanted = jnp.where(lane_row == r, row_prompt[0, r], wanted)
    shared = jnp.where(wanted == 1, din[1], din[0])
    highest = jnp.maximum(shared[136:137], dloc[136:137])
    fa, fb = jnp.exp2(shared[136:137] - highest), jnp.exp2(dloc[136:137] - highest)
    total = shared[128:129] * fa + dloc[128:129] * fb
    o = ((shared[0:128] * fa + dloc[0:128] * fb) / total).T.astype(jnp.bfloat16)
    for h in range(8):
        dout[:, h * 128 : (h + 1) * 128] = o[h * 16 : (h + 1) * 16]

    local.wait()
    for copy in o_copies:
        copy.wait_recv()
    x_copy.wait_send()
    for copy in d_copies + q_copies + r_copies + o_copies:
        copy.wait_send()
    for c in range(4):

        def drain(k, _, c=c):
            ring(k, c).wait_send()
            return 0

        lax.fori_loop(1, half + 1 if c in (0, 3) else half, drain, 0)


def per_device(zs, tps, prompt_query, prompt_kv, block_order, decode_query, history_kv, new_kv, hist_len, row_prompt):
    half = zs // 2
    rows = 128 // tps
    vmem = pl.BlockSpec(memory_space=pltpu.VMEM)
    smem = pl.BlockSpec(memory_space=pltpu.SMEM)
    dma = pltpu.SemaphoreType.DMA
    prefill_out, decode_out = pl.pallas_call(
        functools.partial(kernel, half, tps),
        out_shape=(
            jax.ShapeDtypeStruct((1, 2, rows, 1024 * tps), jnp.bfloat16),
            jax.ShapeDtypeStruct((16, 1024), jnp.bfloat16),
        ),
        in_specs=[smem] * 3 + [vmem] * 5,
        out_specs=(pl.BlockSpec(memory_space=pl.ANY), vmem),
        scratch_shapes=[
            pltpu.VMEM((half + 1, 4, 256, 128), jnp.bfloat16),
            pltpu.VMEM((256, 128), jnp.bfloat16),
            pltpu.VMEM((4, 128, 256), jnp.bfloat16),
            pltpu.VMEM((128, 128), jnp.bfloat16),
            pltpu.VMEM((2, 128, 128), jnp.bfloat16),
            pltpu.VMEM((9, 128 + ONES, 256), jnp.float32),
            pltpu.VMEM((9, 8, 256), jnp.float32),
            pltpu.VMEM((2, 128, 1024), jnp.bfloat16),
            pltpu.VMEM((2, 144, 128), jnp.float32),
            pltpu.VMEM((2, 144, 128), jnp.float32),
            pltpu.VMEM((144, 128), jnp.float32),
            dma((half + 1, 4)),
            dma((half + 1, 4)),
            dma(()),
            dma(()),
            dma((4,)),
            dma((4,)),
            dma((2,)),
            dma((2,)),
            dma((2,)),
            dma((2,)),
            dma((2, tps)),
            dma((2, tps)),
            dma(()),
        ],
        compiler_params=pltpu.CompilerParams(
            collective_id=0, has_side_effects=True, vmem_limit_bytes=48 << 20
        ),
    )(
        block_order,
        hist_len,
        row_prompt,
        prompt_query,
        prompt_kv,
        decode_query.reshape(16, 1024),
        history_kv,
        new_kv.reshape(2, 16, 128),
    )
    return prefill_out, decode_out.reshape(decode_query.shape)


def solution(mesh):
    placed = (
        P("pool", None, "ctx", "tp"),
        P("pool", None, None, "ctx", "tp"),
        P("pool", None, None),
        P("pool", "ctx", None, "tp"),
        P("pool", None, "ctx", None, "tp"),
        P("pool", None, "ctx", None, "tp"),
        P("pool", "ctx"),
        P("pool", "ctx"),
    )
    return jax.shard_map(
        functools.partial(per_device, mesh.shape["ctx"] // 2, mesh.shape["tp"]),
        mesh=mesh,
        in_specs=placed,
        out_specs=(P("pool", None, ("ctx", "tp"), None), P("pool", "ctx", None, "tp")),
        check_vma=False,
    )
```

time: 357 us -> 64.9 us (0.18)
  waiting for transfers between devices: 244 us -> 0 us
  matrix products: 64.7 us -> 0 us
  Pallas kernels: 0 us -> 57.9 us
  other arithmetic: 14.5 us -> 0 us
  between operations: 14.3 us -> 0.72 us
  starting transfers between devices: 6.83 us -> 0 us
  local copies, waits for them, and re-layouts: 11.5 us -> 5.13 us
    all_gather x2 -> x0, waiting for transfers between devices: 243 us -> none  [the longest x1 161 us: per_device(): lax.all_gather(prompt_kv, 'ctx', axis=3, tiled=True)]
    dot_general x22 -> x0, matrix products: 64.7 us -> none  [the longest x8 37.2 us: one_block(): jnp.einsum('pnegm,pmed->pnegd', weights.astype(jnp.bfloat16), rows_of_val...]
    pallas_call x0 -> x1, Pallas kernels: none -> 57.9 us  [per_device(): pl.pallas_call(functools.partial(kernel, half, tps), out_shape=(jax.Shape...]
    reduce_sum x19 -> x0, other arithmetic: 9.54 us -> none  [the longest x8 6.97 us: one_block(): weight_sum = weight_sum * factor + jnp.sum(weights, axis=-1)]
    another operation x3 -> x0, local copies, waits for them, and re-layouts: 5.46 us -> none  [the longest x1 3.88 us: accumulate(): incoming[0, 1].reshape(prompts, key_count, kv_heads, HEAD_SIZE)]
    all_to_all x1 -> x0, starting transfers between devices: 4.83 us -> none  [per_device(): lax.all_to_all(local_out, 'tp', split_axis=2, concat_axis=3, tiled=True)]
  transfers between devices with their start and end apart: 4 -> 0, of which waited for: 2 -> 0; matrix products, arithmetic and copies ran while one was open for 25% -> 0% of each run, Pallas kernels for 0% -> 0%
where the time goes in v1:
time: 64.9 us; the launch traced here: 63.7 us
  Pallas kernels  57.9 us (89%)
  local copies, waits for them, and re-layouts  5.13 us (8%)
  between operations  0.72 us (1%)
    pallas_call x1, Pallas kernels, per_device(): pl.pallas_call(functools.partial(kernel, half, tps), out_shape=(jax.Shape...  57.9 us
    unnamed x15, local copies, waits for them, and re-layouts  3.7 us

profile of v1, /device:TPU:6, one launch (start us, length us, event | category | flops | bytes accessed | tf_op | source)
XLA Modules:
  0.0 63.7 jit_solution(8735757729815388681)
XLA Ops:
  0.6 0.0 copy-start.3
  0.6 0.0 copy-start.4
  0.7 0.0 copy-start.5
  0.7 0.0 copy-start.6
  0.7 0.8 %reshape.13.dq = bf16[16,1024]{1,0:T(8,128)(2,1)S(1)} reshape(bf16[1,8,2,1024]{3,2,1,0:T(2,128)(2,1)} %param.11) | data formatting | bytes 65536 | tf_op jit(solution)/shard_map/reshape | solution.py:394
  1.5 0.0 copy-done.3
  1.5 0.0 copy-done.4
  1.5 0.0 copy-done.5
  1.5 0.0 copy-done.6
  1.5 0.0 copy-start
  1.5 1.0 %copy-done = bf16[1,2,128,1024]{3,2,1,0:T(8,128)(2,1)S(1)} copy-done((bf16[1,2,128,1024]{3,2,1,0:T(8,128)(2,1)S(1)}, bf16[1,2,128,1024]{3,2,1,0:T(8,128)(2,1)}, u32[]{:S(2)}) %copy-start) | copy-done | bytes 524312
  2.6 0.0 copy-start.1
  2.6 0.9 %copy-done.1 = bf16[1,2,8,64,128]{4,3,2,1,0:T(8,128)(2,1)S(1)} copy-done((bf16[1,2,8,64,128]{4,3,2,1,0:T(8,128)(2,1)S(1)}, bf16[1,2,8,64,128]{4,3,2,1,0:T(8,128)(2,1)}, u32[]{:S(2)}) %copy-start.1) | copy-done | bytes 262168
  3.5 0.0 copy-start.2
  3.5 0.9 %copy-done.2 = bf16[1,2,2,128,128]{4,3,2,1,0:T(8,128)(2,1)S(1)} copy-done((bf16[1,2,2,128,128]{4,3,2,1,0:T(8,128)(2,1)S(1)}, bf16[1,2,2,128,128]{4,3,2,1,0:T(8,128)(2,1)}, u32[]{:S(2)}) %copy-start.2) | copy-done | bytes 131096
  4.4 57.9 %shard_map.95 = (bf16[1,2,16,8192]{3,2,1,0:T(8,128)(2,1)S(1)}, bf16[16,1024]{1,0:T(8,128)(2,1)S(1)}) custom-call(s32[1,2,32]{2,1,0:T(2,128)S(1)} %copy-done.4, s32[1,8]{1,0:T(1,128)S(1)} %copy-done.5, s32[1,8]{1,0:T(1,128)S(1)} %copy-done.6, bf16[1,2,128,1024]{3,2,1,0:T(8,128)(2,1)S(1)} %copy-done, bf16[1,2,2,128,128]{4,3,2,1,0:T(8,128)(2,1)S(1)} %copy-done.2, ...), custom_call_target="tpu_custom_call" | custom-call | tf_op jit(solution)/shard_map/pallas_call | solution.py:351
  62.3 0.6 reshape.15
  63.0 0.8 %copy.11 = bf16[1,2,16,8192]{3,2,1,0:T(8,128)(2,1)} copy(bf16[1,2,16,8192]{3,2,1,0:T(8,128)(2,1)S(1)} %get-tuple-element.8) | data formatting | bytes 1048576
Async XLA Ops:
  0.6 0.8 %copy-start.3 = (bf16[1,2,8,2,128]{4,3,2,1,0:T(2,128)(2,1)S(1)}, bf16[1,2,8,2,128]{4,3,2,1,0:T(2,128)(2,1)}, u32[]{:S(2)}) copy-start(bf16[1,2,8,2,128]{4,3,2,1,0:T(2,128)(2,1)} %param.13) | copy-start | bytes 24580
  0.6 0.8 %copy-start.4 = (s32[1,2,32]{2,1,0:T(2,128)S(1)}, s32[1,2,32]{2,1,0:T(2,128)}, u32[]{:S(2)}) copy-start(s32[1,2,32]{2,1,0:T(2,128)} %order.1) | copy-start | bytes 772
  0.7 0.8 %copy-start.5 = (s32[1,8]{1,0:T(1,128)S(1)}, s32[1,8]{1,0:T(1,128)}, u32[]{:S(2)}) copy-start(s32[1,8]{1,0:T(1,128)} %hist_len.1) | copy-start | bytes 100
  0.7 0.8 %copy-start.6 = (s32[1,8]{1,0:T(1,128)S(1)}, s32[1,8]{1,0:T(1,128)}, u32[]{:S(2)}) copy-start(s32[1,8]{1,0:T(1,128)} %row_prompt.1) | copy-start | bytes 100
  1.5 1.0 %copy-start = (bf16[1,2,128,1024]{3,2,1,0:T(8,128)(2,1)S(1)}, bf16[1,2,128,1024]{3,2,1,0:T(8,128)(2,1)}, u32[]{:S(2)}) copy-start(bf16[1,2,128,1024]{3,2,1,0:T(8,128)(2,1)} %pq.1) | copy-start | bytes 1572868
  2.6 0.9 %copy-start.1 = (bf16[1,2,8,64,128]{4,3,2,1,0:T(8,128)(2,1)S(1)}, bf16[1,2,8,64,128]{4,3,2,1,0:T(8,128)(2,1)}, u32[]{:S(2)}) copy-start(bf16[1,2,8,64,128]{4,3,2,1,0:T(8,128)(2,1)} %hist.1) | copy-start | bytes 786436
  3.5 0.9 %copy-start.2 = (bf16[1,2,2,128,128]{4,3,2,1,0:T(8,128)(2,1)S(1)}, bf16[1,2,2,128,128]{4,3,2,1,0:T(8,128)(2,1)}, u32[]{:S(2)}) copy-start(bf16[1,2,2,128,128]{4,3,2,1,0:T(8,128)(2,1)} %pkv.1) | copy-start | bytes 393220

commit v2 on v1

v2 whole, which is shorter than its diff:
```python
import functools

import jax
import jax.numpy as jnp
from jax import lax
from jax.experimental import pallas as pl
from jax.experimental.pallas import tpu as pltpu
from jax.sharding import PartitionSpec as P

HEAD_SIZE = 128
NEG = -1e30
SCALE = 1.4426950408889634 / HEAD_SIZE**0.5
NT = (((1,), (1,)), ((), ()))
TN = (((0,), (0,)), ((), ()))
MESH = pl.DeviceIdType.MESH
ONES = 16


def kernel(
    half,
    tps,
    order_in,
    hist_len_in,
    row_prompt_in,
    pq,
    pkv_in,
    dq_in,
    hist_in,
    new_in,
    out,
    dout,
    order,
    hist_len,
    row_prompt,
    q0,
    raw,
    dq,
    hist,
    new,
    buf,
    psend,
    q1,
    dqs,
    dqr,
    acc,
    top,
    stage,
    dstage,
    din,
    dloc,
    in_sem,
    ring_send,
    ring_recv,
    x_send,
    x_recv,
    near_send,
    q_send,
    q_recv,
    d_send,
    d_recv,
    r_send,
    r_recv,
    o_send,
    o_recv,
    o_local,
):
    ctx, tp, core = lax.axis_index("ctx"), lax.axis_index("tp"), lax.axis_index("pool")
    zs = 2 * half
    z, yh = ctx // 2, ctx % 2
    rows = 128 // tps

    def dev(z_, yh_, tp_, core_):
        return {"ctx": lax.rem(z_ + zs, zs) * 2 + yh_, "tp": tp_, "pool": core_}

    right, left = dev(z + 1, yh, tp, core), dev(z - 1, yh, tp, core)
    partner = dev(z, 1 - yh, tp, core)
    partner_right, partner_left = dev(z + 1, 1 - yh, tp, core), dev(z - 1, 1 - yh, tp, core)
    helpers = (dev(z, yh, tp, 1 - core), dev(z, 1 - yh, tp, 1 - core))

    def other_tp(k):
        return lax.rem(tp + k, tps)

    owners = [[dev(z, yh, other_tp(k), core) for k in range(tps)], [dev(z, 1 - yh, other_tp(k), core) for k in range(tps)]]

    def remote(src, dst, send, recv, device):
        return pltpu.make_async_remote_copy(
            src_ref=src, dst_ref=dst, send_sem=send, recv_sem=recv, device_id=device, device_id_type=MESH
        )

    barrier = pltpu.get_barrier_semaphore()
    peers = [right, left, partner_right, partner_left, *helpers, *owners[0][1:], *owners[1]]
    for peer in peers:
        pl.semaphore_signal(barrier, inc=1, device_id=peer, device_id_type=MESH)

    fetches = [
        pltpu.make_async_copy(src, dst, in_sem.at[i])
        for i, (src, dst) in enumerate(
            [
                (pkv_in.at[0, 1], raw),
                (dq_in.at[0], dq),
                (pkv_in.at[0, 0, yh], buf.at[0, 0, 0:128]),
                (hist_len_in, hist_len),
                (hist_in.at[0], hist),
                (new_in, new),
                (order_in, order),
                (row_prompt_in, row_prompt),
                (pq.at[0, yh], q0),
            ]
        )
    ]
    for fetch in fetches:
        fetch.start()
    pl.semaphore_wait(barrier, len(peers))

    def part(ref, h):
        return ref.at[h * 128 : (h + 1) * 128]

    def ring(k, c, h, src=None):
        return remote(
            part(buf.at[k - 1, c], h) if src is None else src,
            part(buf.at[k, c], h),
            ring_send.at[k, c, h],
            ring_recv.at[k, c, h],
            right if c < 2 else left,
        )

    mine = (pkv_in.at[0, 0, yh], part(buf.at[0, 0], 1))
    theirs = (pkv_in.at[0, 0, 1 - yh], psend)
    x_copies = [remote(theirs[h], part(buf.at[0, 1], h), x_send.at[h], x_recv.at[h], partner) for h in range(2)]
    near_copies = [
        [
            remote(theirs[h], part(buf.at[1, c], h), near_send.at[i, h], ring_recv.at[1, c, h], device)
            for i, (c, device) in enumerate([(1, partner_right), (3, partner_left)])
        ]
        for h in range(2)
    ]
    q_copy = remote(pq.at[0, 1 - yh], q1, q_send, q_recv, partner)
    d_copies = [remote(dqs, dqr.at[i], d_send.at[i], d_recv.at[i], helpers[i]) for i in range(2)]
    def send_own(h):
        for copy in [ring(1, 0, h, mine[h]), ring(1, 2, h, mine[h]), *near_copies[h], x_copies[h]]:
            copy.start()

    send_own(0)
    fetches[0].wait()
    buf[0, 0, 128:256, :] = raw[yh].astype(jnp.float32).T.astype(jnp.bfloat16)
    psend[...] = raw[1 - yh].astype(jnp.float32).T.astype(jnp.bfloat16)
    send_own(1)
    fetches[1].wait()
    wide = dq[...].astype(jnp.float32).reshape(16, 1024)
    dqt = jnp.concatenate([wide[:, h * 128 : (h + 1) * 128] for h in range(8)], axis=0).astype(jnp.bfloat16)
    dqs[...] = dqt
    for copy in d_copies:
        copy.start()
    for fetch in fetches[2:]:
        fetch.wait()

    lane = lax.broadcasted_iota(jnp.int32, (1, 128), 1)
    lane_row, lane_step = lax.rem(lane, 16) // 2, lax.rem(lane, 2)
    hs = lax.dot_general(hist[0].reshape(512, 128), dqt, NT, preferred_element_type=jnp.float32) * SCALE
    key_in_row = lax.broadcasted_iota(jnp.int32, (64, 128), 0)
    hs = jnp.concatenate(
        [
            jnp.where((lane_row == r) & (key_in_row < hist_len[0, r]), hs[r * 64 : (r + 1) * 64], NEG)
            for r in range(8)
        ],
        axis=0,
    )
    ns = lax.dot_general(new[0], dqt, NT, preferred_element_type=jnp.float32) * SCALE
    key = lax.broadcasted_iota(jnp.int32, (16, 128), 0)
    ns = jnp.where((key // 2 == lane_row) & (lax.rem(key, 2) <= lane_step), ns, NEG)
    highest = jnp.maximum(jnp.max(hs, axis=0, keepdims=True), jnp.max(ns, axis=0, keepdims=True))
    hw, nw = jnp.exp2(hs - highest), jnp.exp2(ns - highest)
    weighted = lax.dot_general(
        hist[1].reshape(512, 128), hw.astype(jnp.bfloat16), TN, preferred_element_type=jnp.float32
    ) + lax.dot_general(new[1], nw.astype(jnp.bfloat16), TN, preferred_element_type=jnp.float32)
    dloc[0:128] = weighted
    dloc[128:136] = jnp.broadcast_to(jnp.sum(hw, 0, keepdims=True) + jnp.sum(nw, 0, keepdims=True), (8, 128))
    dloc[136:144] = jnp.broadcast_to(highest, (8, 128))

    def event(k, b, h, last=0):
        for c in (b, b + 2):
            if last < 2 or c in (0, 3):
                ring(k, c, h).wait_recv()
                if last == 0 or (last == 1 and c in (0, 3)):
                    ring(k + 1, c, h).start()

    def queries(t):
        if t == 8:
            return dqr[...].reshape(256, 128)
        x = (q0 if t < 4 else q1)[:, t % 4 * 256 : (t % 4 + 1) * 256]
        return jnp.concatenate([x[:, :128], x[:, 128:]], axis=0)

    causal = lax.rem(lax.broadcasted_iota(jnp.int32, (128, 256), 1), 128) >= lax.broadcasted_iota(
        jnp.int32, (128, 256), 0
    )

    def place(z_, yh_):
        return order[0, yh, lax.rem(z_ + zs, zs) * 2 + yh_]

    own_place = (place(z, yh), place(z, 1 - yh))

    def attend(tiles, u, chunks, sources, first=False, between=()):
        between = dict(between)
        keys = jnp.concatenate([buf[u, c, 0:128, :] for c in chunks], axis=0)
        values = jnp.concatenate(
            [
                jnp.concatenate([buf[u, c, 128:256, :] for c in chunks], axis=1),
                jnp.ones((ONES, 128 * len(chunks)), jnp.bfloat16),
            ],
            axis=0,
        )
        places = [place(*s) for s in sources]
        bias = [[jnp.where(pk <= own_place[i], 0.0, NEG).astype(jnp.float32) for pk in places] for i in range(2)]

        def scores(t):
            return lax.dot_general(keys, queries(t), NT, preferred_element_type=jnp.float32)

        def weights(t, s):
            s = s * SCALE
            parts = [s[i * 128 : (i + 1) * 128] for i in range(len(chunks))]
            shift = [None] * len(chunks)
            if t < 8:
                shift = list(bias[t // 4])
                if first:
                    shift[t // 4] = None
                    parts[t // 4] = jnp.where(causal, parts[t // 4], NEG)
            tops = [jnp.max(x, axis=0, keepdims=True) for x in parts]
            tops = [x if b is None else x + b for x, b in zip(tops, shift)]
            now = functools.reduce(jnp.maximum, tops)
            factor = None
            if not first:
                before = top[t, 0:1]
                now = jnp.maximum(now, before)
                factor = jnp.exp2(before - now)
            top[t, 0:1] = now
            w = [jnp.exp2(x - (now if b is None else now - b)).astype(jnp.bfloat16) for x, b in zip(parts, shift)]
            return jnp.concatenate(w, axis=0), factor

        def add(t, w, factor):
            o = jnp.dot(values, w, preferred_element_type=jnp.float32)
            acc[t] = o if factor is None else acc[t] * factor + o

        s = {i: scores(tiles[i]) for i in range(min(2, len(tiles)))}
        w = {0: weights(tiles[0], s[0])}
        for i in range(len(tiles)):
            if i in between:
                event(*between[i])
            if i + 2 < len(tiles):
                s[i + 2] = scores(tiles[i + 2])
            if i + 1 < len(tiles):
                w[i + 1] = weights(tiles[i + 1], s[i + 1])
            add(tiles[i], *w[i])

    def own(tiles):
        attend(tiles, 0, (0, 1), [(z, yh), (z, 1 - yh)], first=True)

    def step(k, tiles, between=()):
        attend(tiles, k, (0, 1, 2, 3), [(z - k, yh), (z - k, 1 - yh), (z + k, yh), (z + k, 1 - yh)], between=between)

    event(1, 0, 0)
    event(1, 0, 1)
    event(1, 1, 0)
    event(1, 1, 1)
    for copy in x_copies:
        copy.wait_recv()
    q_copy.start()
    for copy in d_copies:
        copy.wait_recv()
    own([0, 1, 2, 3, 8])
    def at(k, places, last=0):
        return [(i, (k, b, h, last)) for i, (b, h) in zip(places, [(0, 0), (0, 1), (1, 0), (1, 1)])]

    early, late = [0, 1, 2, 3, 8], [4, 5, 6, 7]
    everything = [8, 4, 5, 6, 7, 0, 1, 2, 3]
    step(1, early, at(2, (1, 2, 3, 4)))
    step(2, early, at(3, (1, 2, 3, 4)))
    q_copy.wait_recv()
    own(late)
    step(1, late)
    step(2, late, [(1, (4, 0, 0)), (3, (4, 0, 1))])
    step(3, everything, [(1, (4, 1, 0)), (3, (4, 1, 1))])

    def middle_step(k, _):
        step(k, everything, at(k + 1, (2, 4, 6, 8)))
        return 0

    lax.fori_loop(4, half - 2, middle_step, 0)
    step(half - 2, everything, at(half - 1, (2, 4, 6, 8), 1))
    step(half - 1, everything)
    for b in range(2):
        for h in range(2):
            event(half, b, h, 2)

    far = [(z - half, yh), (z + half, 1 - yh)]
    attend([8, 4, 5, 6, 7], half, (0, 3), far)
    r_copies = []
    for i in range(2):
        dstage[i, 0:136] = acc[8, 0:136, i * 128 : (i + 1) * 128]
        dstage[i, 136:144] = jnp.broadcast_to(top[8, 0:1, i * 128 : (i + 1) * 128], (8, 128))
        r_copies.append(remote(dstage.at[i], din.at[yh], r_send.at[i], r_recv.at[i], helpers[i]))
        r_copies[i].start()

    o_copies = []
    for item in (1, 0):
        if item == 0:
            attend([0, 1, 2, 3], half, (0, 3), far)
        for t in range(4):
            a = acc[item * 4 + t]
            o = a[0:128] * (1.0 / a[128:129])
            for h in range(2):
                col = (2 * t + h) * 128
                stage[item, :, col : col + 128] = o[:, h * 128 : (h + 1) * 128].T.astype(jnp.bfloat16)
        for k in range(tps):
            src = stage.at[item, pl.ds(pl.multiple_of(other_tp(k) * rows, rows), rows), :]
            dst = out.at[0, yh, :, pl.ds(pl.multiple_of(tp * 1024, 1024), 1024)]
            if item == 0 and k == 0:
                local = pltpu.make_async_copy(src, dst, o_local)
                local.start()
            else:
                o_copies.append(remote(src, dst, o_send.at[item, k], o_recv.at[item, k], owners[item][k]))
                o_copies[-1].start()

    for copy in r_copies:
        copy.wait_recv()
    wanted = jnp.zeros((1, 128), jnp.int32)
    for r in range(8):
        wanted = jnp.where(lane_row == r, row_prompt[0, r], wanted)
    shared = jnp.where(wanted == 1, din[1], din[0])
    highest = jnp.maximum(shared[136:137], dloc[136:137])
    fa, fb = jnp.exp2(shared[136:137] - highest), jnp.exp2(dloc[136:137] - highest)
    total = shared[128:129] * fa + dloc[128:129] * fb
    o = ((shared[0:128] * fa + dloc[0:128] * fb) * (1.0 / total)).T.astype(jnp.bfloat16)
    for h in range(8):
        dout[:, h * 128 : (h + 1) * 128] = o[h * 16 : (h + 1) * 16]

    for copy in x_copies + near_copies[0] + near_copies[1] + d_copies + [q_copy] + r_copies:
        copy.wait_send()
    for c in range(4):

        def drain(k, _, c=c):
            for h in range(2):
                ring(k, c, h).wait_send()
            return 0

        lax.fori_loop(1 if c in (0, 2) else 2, half + 1 if c in (0, 3) else half, drain, 0)
    local.wait()
    for copy in o_copies:
        copy.wait()


def finish(prefill, decode, prefill_out, decode_out, held, rows, shaped, in_sem, out_sem):
    pieces = prefill.shape[1]
    moves = [
        (
            pltpu.make_async_copy(prefill.at[0, i], held.at[i], in_sem.at[i]),
            pltpu.make_async_copy(held.at[i], prefill_out.at[0, i], out_sem.at[i]),
        )
        for i in range(pieces)
    ]
    moves.append(
        (
            pltpu.make_async_copy(decode, rows, in_sem.at[pieces]),
            pltpu.make_async_copy(shaped, decode_out.at[0], out_sem.at[pieces]),
        )
    )
    for load, _ in moves:
        load.start()
    for load, store in moves[:-1]:
        load.wait()
        store.start()
    load, store = moves[-1]
    load.wait()
    shaped[...] = rows[...].astype(jnp.float32).reshape(shaped.shape).astype(jnp.bfloat16)
    store.start()
    for _, store in moves:
        store.wait()


def per_device(zs, tps, prompt_query, prompt_kv, block_order, decode_query, history_kv, new_kv, hist_len, row_prompt):
    half = zs // 2
    rows = 128 // tps
    vmem = pl.BlockSpec(memory_space=pltpu.VMEM)
    anywhere = pl.BlockSpec(memory_space=pl.ANY)
    dma = pltpu.SemaphoreType.DMA
    prefill_out, decode_out = pl.pallas_call(
        functools.partial(kernel, half, tps),
        out_shape=(
            jax.ShapeDtypeStruct((1, 2, rows, 1024 * tps), jnp.bfloat16),
            jax.ShapeDtypeStruct((16, 1024), jnp.bfloat16),
        ),
        in_specs=[anywhere] * 8,
        out_specs=(anywhere, vmem),
        scratch_shapes=[
            pltpu.SMEM(block_order.shape, jnp.int32),
            pltpu.SMEM(hist_len.shape, jnp.int32),
            pltpu.SMEM(row_prompt.shape, jnp.int32),
            pltpu.VMEM((128, 1024), jnp.bfloat16),
            pltpu.VMEM((2, 128, 128), jnp.bfloat16),
            pltpu.VMEM((8, 2, 1024), jnp.bfloat16),
            pltpu.VMEM((2, 8, 64, 128), jnp.bfloat16),
            pltpu.VMEM((2, 16, 128), jnp.bfloat16),
            pltpu.VMEM((half + 1, 4, 256, 128), jnp.bfloat16),
            pltpu.VMEM((128, 128), jnp.bfloat16),
            pltpu.VMEM((128, 1024), jnp.bfloat16),
            pltpu.VMEM((128, 128), jnp.bfloat16),
            pltpu.VMEM((2, 128, 128), jnp.bfloat16),
            pltpu.VMEM((9, 128 + ONES, 256), jnp.float32),
            pltpu.VMEM((9, 8, 256), jnp.float32),
            pltpu.VMEM((2, 128, 1024), jnp.bfloat16),
            pltpu.VMEM((2, 144, 128), jnp.float32),
            pltpu.VMEM((2, 144, 128), jnp.float32),
            pltpu.VMEM((144, 128), jnp.float32),
            dma((9,)),
            dma((half + 1, 4, 2)),
            dma((half + 1, 4, 2)),
            dma((2,)),
            dma((2,)),
            dma((2, 2)),
            dma(()),
            dma(()),
            dma((2,)),
            dma((2,)),
            dma((2,)),
            dma((2,)),
            dma((2, tps)),
            dma((2, tps)),
            dma(()),
        ],
        compiler_params=pltpu.CompilerParams(
            collective_id=0, has_side_effects=True, vmem_limit_bytes=63_400_000
        ),
    )(
        block_order,
        hist_len,
        row_prompt,
        prompt_query,
        prompt_kv,
        decode_query,
        history_kv,
        new_kv.reshape(2, 16, 128),
    )
    return pl.pallas_call(
        finish,
        out_shape=(
            jax.ShapeDtypeStruct(prefill_out.shape, jnp.bfloat16),
            jax.ShapeDtypeStruct(decode_query.shape, jnp.bfloat16),
        ),
        in_specs=[anywhere] * 2,
        out_specs=(anywhere, anywhere),
        scratch_shapes=[
            pltpu.VMEM(prefill_out.shape[1:], jnp.bfloat16),
            pltpu.VMEM(decode_out.shape, jnp.bfloat16),
            pltpu.VMEM(decode_query.shape[1:], jnp.bfloat16),
            dma((3,)),
            dma((3,)),
        ],
    )(prefill_out, decode_out)


def solution(mesh):
    placed = (
        P("pool", None, "ctx", "tp"),
        P("pool", None, None, "ctx", "tp"),
        P("pool", None, None),
        P("pool", "ctx", None, "tp"),
        P("pool", None, "ctx", None, "tp"),
        P("pool", None, "ctx", None, "tp"),
        P("pool", "ctx"),
        P("pool", "ctx"),
    )
    return jax.shard_map(
        functools.partial(per_device, mesh.shape["ctx"] // 2, mesh.shape["tp"]),
        mesh=mesh,
        in_specs=placed,
        out_specs=(P("pool", None, ("ctx", "tp"), None), P("pool", "ctx", None, "tp")),
        check_vma=False,
    )
```

time: 64.9 us -> 59.8 us (0.921)
  the two profiles are of different devices: /device:TPU:6 before, /device:TPU:1 now
where the time goes in v2:
time: 59.8 us; the launch traced here: 59.7 us
  Pallas kernels  58.9 us (98%)
  between operations  0.8 us (1%)
    pallas_call x1, Pallas kernels, per_device(): pl.pallas_call(functools.partial(kernel, half, tps), out_shape=(jax.Shape...  57.1 us
    pallas_call x1, Pallas kernels, per_device(): pl.pallas_call(finish, out_shape=(jax.ShapeDtypeStruct(prefill_out.shape,...  1.79 us

profile of v2, /device:TPU:1, one launch (start us, length us, event | category | flops | bytes accessed | tf_op | source)
XLA Modules:
  0.0 59.7 jit_solution(1698094082710794401)
XLA Ops:
  0.6 57.1 %shard_map.95 = (bf16[1,2,16,8192]{3,2,1,0:T(8,128)(2,1)}, bf16[16,1024]{1,0:T(8,128)(2,1)}) custom-call(s32[1,2,32]{2,1,0:T(2,128)} %order_in.1, s32[1,8]{1,0:T(1,128)} %hist_len_in.1, s32[1,8]{1,0:T(1,128)} %row_prompt_in.1, bf16[1,2,128,1024]{3,2,1,0:T(8,128)(2,1)} %pq.1, bf16[1,2,2,128,128]{4,3,2,1,0:T(8,128)(2,1)} %pkv_in.1, ...), custom_call_target="tpu_custom_call" | custom-call | tf_op jit(solution)/shard_map/pallas_call | solution.py:385
  57.7 1.8 %shard_map.96 = (bf16[1,2,16,8192]{3,2,1,0:T(8,128)(2,1)}, bf16[1,8,2,1024]{3,2,1,0:T(2,128)(2,1)}) custom-call(bf16[1,2,16,8192]{3,2,1,0:T(8,128)(2,1)} %get-tuple-element.4.prefill, bf16[16,1024]{1,0:T(8,128)(2,1)} %get-tuple-element.5.decode), custom_call_target="tpu_custom_call" | custom-call | tf_op jit(solution)/shard_map/pallas_call | solution.py:442

commit v3 on v2

--- a/solution.py
+++ b/solution.py
@@ -63,6 +63,7 @@
     o_send,
     o_recv,
     o_local,
+    hello,
 ):
     ctx, tp, core = lax.axis_index("ctx"), lax.axis_index("tp"), lax.axis_index("pool")
     zs = 2 * half
@@ -86,11 +87,6 @@
         return pltpu.make_async_remote_copy(
             src_ref=src, dst_ref=dst, send_sem=send, recv_sem=recv, device_id=device, device_id_type=MESH
         )
-
-    barrier = pltpu.get_barrier_semaphore()
-    peers = [right, left, partner_right, partner_left, *helpers, *owners[0][1:], *owners[1]]
-    for peer in peers:
-        pl.semaphore_signal(barrier, inc=1, device_id=peer, device_id_type=MESH)
 
     fetches = [
         pltpu.make_async_copy(src, dst, in_sem.at[i])
@@ -110,6 +106,13 @@
     ]
     for fetch in fetches:
         fetch.start()
+
+    barrier = pltpu.get_barrier_semaphore()
+    beside = [dev(z, yh, lax.rem(tp + k, tps), core) for k in (2, 6)] + [dev(z, yh, tp + 1 - 2 * (tp % 2), core), partner]
+    peers = [right, left, partner_right, partner_left, *helpers, *beside]
+    for peer in peers:
+        pl.semaphore_signal(barrier, inc=1, device_id=peer, device_id_type=MESH)
+
     pl.semaphore_wait(barrier, len(peers))
 
     def part(ref, h):
@@ -136,6 +139,13 @@
     ]
     q_copy = remote(pq.at[0, 1 - yh], q1, q_send, q_recv, partner)
     d_copies = [remote(dqs, dqr.at[i], d_send.at[i], d_recv.at[i], helpers[i]) for i in range(2)]
+    def greet(i):
+        if i:
+            pl.semaphore_wait(hello.at[i - 1], len(beside))
+        if i < 3:
+            for peer in beside:
+                pl.semaphore_signal(hello.at[i], inc=1, device_id=peer, device_id_type=MESH)
+
     def send_own(h):
         for copy in [ring(1, 0, h, mine[h]), ring(1, 2, h, mine[h]), *near_copies[h], x_copies[h]]:
             copy.start()
@@ -145,6 +155,7 @@
     buf[0, 0, 128:256, :] = raw[yh].astype(jnp.float32).T.astype(jnp.bfloat16)
     psend[...] = raw[1 - yh].astype(jnp.float32).T.astype(jnp.bfloat16)
     send_own(1)
+    greet(0)
     fetches[1].wait()
     wide = dq[...].astype(jnp.float32).reshape(16, 1024)
     dqt = jnp.concatenate([wide[:, h * 128 : (h + 1) * 128] for h in range(8)], axis=0).astype(jnp.bfloat16)
@@ -257,10 +268,9 @@
     def step(k, tiles, between=()):
         attend(tiles, k, (0, 1, 2, 3), [(z - k, yh), (z - k, 1 - yh), (z + k, yh), (z + k, 1 - yh)], between=between)
 
-    event(1, 0, 0)
-    event(1, 0, 1)
-    event(1, 1, 0)
-    event(1, 1, 1)
+    for h in range(2):
+        for b in range(2):
+            event(1, b, h)
     for copy in x_copies:
         copy.wait_recv()
     q_copy.start()
@@ -268,17 +278,19 @@
         copy.wait_recv()
     own([0, 1, 2, 3, 8])
     def at(k, places, last=0):
-        return [(i, (k, b, h, last)) for i, (b, h) in zip(places, [(0, 0), (0, 1), (1, 0), (1, 1)])]
+        return [(i, (k, b, h, last)) for i, (b, h) in zip(places, [(0, 0), (1, 0), (0, 1), (1, 1)])]
 
     early, late = [0, 1, 2, 3, 8], [4, 5, 6, 7]
     everything = [8, 4, 5, 6, 7, 0, 1, 2, 3]
     step(1, early, at(2, (1, 2, 3, 4)))
+    greet(1)
     step(2, early, at(3, (1, 2, 3, 4)))
     q_copy.wait_recv()
     own(late)
     step(1, late)
-    step(2, late, [(1, (4, 0, 0)), (3, (4, 0, 1))])
-    step(3, everything, [(1, (4, 1, 0)), (3, (4, 1, 1))])
+    greet(2)
+    step(2, late, at(4, (1, 3)))
+    step(3, everything, [(1, (4, 0, 1)), (3, (4, 1, 1))])
 
     def middle_step(k, _):
         step(k, everything, at(k + 1, (2, 4, 6, 8)))
@@ -301,15 +313,16 @@
         r_copies[i].start()
 
     o_copies = []
+    greet(3)
     for item in (1, 0):
         if item == 0:
             attend([0, 1, 2, 3], half, (0, 3), far)
         for t in range(4):
             a = acc[item * 4 + t]
-            o = a[0:128] * (1.0 / a[128:129])
+            o = (a[0:128] * (1.0 / a[128:129])).astype(jnp.bfloat16)
             for h in range(2):
                 col = (2 * t + h) * 128
-                stage[item, :, col : col + 128] = o[:, h * 128 : (h + 1) * 128].T.astype(jnp.bfloat16)
+                stage[item, :, col : col + 128] = o[:, h * 128 : (h + 1) * 128].T
         for k in range(tps):
             src = stage.at[item, pl.ds(pl.multiple_of(other_tp(k) * rows, rows), rows), :]
             dst = out.at[0, yh, :, pl.ds(pl.multiple_of(tp * 1024, 1024), 1024)]
@@ -425,6 +438,7 @@
             dma((2, tps)),
             dma((2, tps)),
             dma(()),
+            pltpu.SemaphoreType.REGULAR((3,)),
         ],
         compiler_params=pltpu.CompilerParams(
             collective_id=0, has_side_effects=True, vmem_limit_bytes=63_400_000

time: 59.8 us -> 58.5 us (0.978)
  the two profiles are of different devices: /device:TPU:1 before, /device:TPU:6 now
where the time goes in v3:
time: 58.5 us; the launch traced here: 58.3 us
  Pallas kernels  57.5 us (98%)
  between operations  0.8 us (1%)
    pallas_call x1, Pallas kernels, per_device(): pl.pallas_call(functools.partial(kernel, half, tps), out_shape=(jax.Shape...  55.7 us
    pallas_call x1, Pallas kernels, per_device(): pl.pallas_call(finish, out_shape=(jax.ShapeDtypeStruct(prefill_out.shape,...  1.79 us

profile of v3, /device:TPU:6, one launch (start us, length us, event | category | flops | bytes accessed | tf_op | source)
XLA Modules:
  0.0 58.3 jit_solution(15888186385857847161)
XLA Ops:
  0.6 55.7 %shard_map.95 = (bf16[1,2,16,8192]{3,2,1,0:T(8,128)(2,1)}, bf16[16,1024]{1,0:T(8,128)(2,1)}) custom-call(s32[1,2,32]{2,1,0:T(2,128)} %order_in.1, s32[1,8]{1,0:T(1,128)} %hist_len_in.1, s32[1,8]{1,0:T(1,128)} %row_prompt_in.1, bf16[1,2,128,1024]{3,2,1,0:T(8,128)(2,1)} %pq.1, bf16[1,2,2,128,128]{4,3,2,1,0:T(8,128)(2,1)} %pkv_in.1, ...), custom_call_target="tpu_custom_call" | custom-call | tf_op jit(solution)/shard_map/pallas_call | solution.py:398
  56.3 1.8 %shard_map.96 = (bf16[1,2,16,8192]{3,2,1,0:T(8,128)(2,1)}, bf16[1,8,2,1024]{3,2,1,0:T(2,128)(2,1)}) custom-call(bf16[1,2,16,8192]{3,2,1,0:T(8,128)(2,1)} %get-tuple-element.4.prefill, bf16[16,1024]{1,0:T(8,128)(2,1)} %get-tuple-element.5.decode), custom_call_target="tpu_custom_call" | custom-call | tf_op jit(solution)/shard_map/pallas_call | solution.py:456

commit v4 on v3

--- a/solution.py
+++ b/solution.py
@@ -64,6 +64,8 @@
     o_recv,
     o_local,
     hello,
+    dheld,
+    dout_sem,
 ):
     ctx, tp, core = lax.axis_index("ctx"), lax.axis_index("tp"), lax.axis_index("pool")
     zs = 2 * half
@@ -210,7 +212,7 @@
 
     own_place = (place(z, yh), place(z, 1 - yh))
 
-    def attend(tiles, u, chunks, sources, first=False, between=()):
+    def attend(tiles, u, chunks, sources, first=False, between=(), after=None):
         between = dict(between)
         keys = jnp.concatenate([buf[u, c, 0:128, :] for c in chunks], axis=0)
         values = jnp.concatenate(
@@ -261,6 +263,8 @@
             if i + 1 < len(tiles):
                 w[i + 1] = weights(tiles[i + 1], s[i + 1])
             add(tiles[i], *w[i])
+            if after:
+                after(tiles[i])
 
     def own(tiles):
         attend(tiles, 0, (0, 1), [(z, yh), (z, 1 - yh)], first=True)
@@ -271,9 +275,10 @@
     for h in range(2):
         for b in range(2):
             event(1, b, h)
+        if h == 0:
+            q_copy.start()
     for copy in x_copies:
         copy.wait_recv()
-    q_copy.start()
     for copy in d_copies:
         copy.wait_recv()
     own([0, 1, 2, 3, 8])
@@ -287,51 +292,55 @@
     step(2, early, at(3, (1, 2, 3, 4)))
     q_copy.wait_recv()
     own(late)
-    step(1, late)
+    step(1, late, at(4, (1, 3)))
     greet(2)
-    step(2, late, at(4, (1, 3)))
-    step(3, everything, [(1, (4, 0, 1)), (3, (4, 1, 1))])
+    step(2, late, [(1, (4, 0, 1)), (3, (4, 1, 1))])
+    step(3, everything, at(5, (1, 3, 5, 7)))
 
     def middle_step(k, _):
-        step(k, everything, at(k + 1, (2, 4, 6, 8)))
+        step(k, everything, at(k + 2, (1, 3, 5, 7)))
         return 0
 
-    lax.fori_loop(4, half - 2, middle_step, 0)
-    step(half - 2, everything, at(half - 1, (2, 4, 6, 8), 1))
+    lax.fori_loop(4, half - 3, middle_step, 0)
+    step(half - 3, everything, at(half - 1, (1, 3, 5, 7), 1))
+    step(half - 2, everything)
     step(half - 1, everything)
     for b in range(2):
         for h in range(2):
             event(half, b, h, 2)
 
     far = [(z - half, yh), (z + half, 1 - yh)]
-    attend([8, 4, 5, 6, 7], half, (0, 3), far)
-    r_copies = []
-    for i in range(2):
-        dstage[i, 0:136] = acc[8, 0:136, i * 128 : (i + 1) * 128]
-        dstage[i, 136:144] = jnp.broadcast_to(top[8, 0:1, i * 128 : (i + 1) * 128], (8, 128))
-        r_copies.append(remote(dstage.at[i], din.at[yh], r_send.at[i], r_recv.at[i], helpers[i]))
-        r_copies[i].start()
-
-    o_copies = []
-    greet(3)
-    for item in (1, 0):
-        if item == 0:
-            attend([0, 1, 2, 3], half, (0, 3), far)
-        for t in range(4):
-            a = acc[item * 4 + t]
-            o = (a[0:128] * (1.0 / a[128:129])).astype(jnp.bfloat16)
-            for h in range(2):
-                col = (2 * t + h) * 128
-                stage[item, :, col : col + 128] = o[:, h * 128 : (h + 1) * 128].T
+    r_copies, o_copies, local = [], [], []
+
+    def deliver(t):
+        if t == 8:
+            for i in range(2):
+                dstage[i, 0:136] = acc[8, 0:136, i * 128 : (i + 1) * 128]
+                dstage[i, 136:144] = jnp.broadcast_to(top[8, 0:1, i * 128 : (i + 1) * 128], (8, 128))
+                r_copies.append(remote(dstage.at[i], din.at[yh], r_send.at[i], r_recv.at[i], helpers[i]))
+                r_copies[i].start()
+            return
+        item = t // 4
+        a = acc[t]
+        o = (a[0:128] * (1.0 / a[128:129])).astype(jnp.bfloat16)
+        for h in range(2):
+            col = (2 * (t % 4) + h) * 128
+            stage[item, :, col : col + 128] = o[:, h * 128 : (h + 1) * 128].T
+        if t == 7:
+            greet(3)
+        if t % 4 < 3:
+            return
         for k in range(tps):
             src = stage.at[item, pl.ds(pl.multiple_of(other_tp(k) * rows, rows), rows), :]
             dst = out.at[0, yh, :, pl.ds(pl.multiple_of(tp * 1024, 1024), 1024)]
             if item == 0 and k == 0:
-                local = pltpu.make_async_copy(src, dst, o_local)
-                local.start()
+                local.append(pltpu.make_async_copy(src, dst, o_local))
+                local[0].start()
             else:
                 o_copies.append(remote(src, dst, o_send.at[item, k], o_recv.at[item, k], owners[item][k]))
                 o_copies[-1].start()
+
+    attend(everything, half, (0, 3), far, after=deliver)
 
     for copy in r_copies:
         copy.wait_recv()
@@ -342,9 +351,11 @@
     highest = jnp.maximum(shared[136:137], dloc[136:137])
     fa, fb = jnp.exp2(shared[136:137] - highest), jnp.exp2(dloc[136:137] - highest)
     total = shared[128:129] * fa + dloc[128:129] * fb
-    o = ((shared[0:128] * fa + dloc[0:128] * fb) * (1.0 / total)).T.astype(jnp.bfloat16)
-    for h in range(8):
-        dout[:, h * 128 : (h + 1) * 128] = o[h * 16 : (h + 1) * 16]
+    o = ((shared[0:128] * fa + dloc[0:128] * fb) * (1.0 / total)).T
+    o = jnp.concatenate([o[h * 16 : (h + 1) * 16] for h in range(8)], axis=1)
+    dheld[...] = o.reshape(dheld.shape).astype(jnp.bfloat16)
+    d_out = pltpu.make_async_copy(dheld, dout, dout_sem)
+    d_out.start()
 
     for copy in x_copies + near_copies[0] + near_copies[1] + d_copies + [q_copy] + r_copies:
         copy.wait_send()
@@ -356,53 +367,42 @@
             return 0
 
         lax.fori_loop(1 if c in (0, 2) else 2, half + 1 if c in (0, 3) else half, drain, 0)
-    local.wait()
+    local[0].wait()
+    d_out.wait()
     for copy in o_copies:
         copy.wait()
 
 
-def finish(prefill, decode, prefill_out, decode_out, held, rows, shaped, in_sem, out_sem):
-    pieces = prefill.shape[1]
-    moves = [
-        (
-            pltpu.make_async_copy(prefill.at[0, i], held.at[i], in_sem.at[i]),
-            pltpu.make_async_copy(held.at[i], prefill_out.at[0, i], out_sem.at[i]),
-        )
-        for i in range(pieces)
-    ]
-    moves.append(
-        (
-            pltpu.make_async_copy(decode, rows, in_sem.at[pieces]),
-            pltpu.make_async_copy(shaped, decode_out.at[0], out_sem.at[pieces]),
-        )
-    )
-    for load, _ in moves:
+def finish(prefill, decode, prefill_out, decode_out, held, rows, in_sem, out_sem):
+    half = prefill.shape[3] // 2
+    moves = [(decode, rows, decode_out.at[0])]
+    for i in range(4):
+        piece = (i // 2, slice(None), pl.ds(i % 2 * half, half))
+        moves.append((prefill.at[(0, *piece)], held.at[piece], prefill_out.at[(0, *piece)]))
+    loads = [pltpu.make_async_copy(src, via, in_sem.at[i]) for i, (src, via, _) in enumerate(moves)]
+    stores = [pltpu.make_async_copy(via, dst, out_sem.at[i]) for i, (_, via, dst) in enumerate(moves)]
+    for load in loads:
         load.start()
-    for load, store in moves[:-1]:
+    for load, store in zip(loads, stores):
         load.wait()
         store.start()
-    load, store = moves[-1]
-    load.wait()
-    shaped[...] = rows[...].astype(jnp.float32).reshape(shaped.shape).astype(jnp.bfloat16)
-    store.start()
-    for _, store in moves:
+    for store in stores:
         store.wait()
 
 
 def per_device(zs, tps, prompt_query, prompt_kv, block_order, decode_query, history_kv, new_kv, hist_len, row_prompt):
     half = zs // 2
     rows = 128 // tps
-    vmem = pl.BlockSpec(memory_space=pltpu.VMEM)
     anywhere = pl.BlockSpec(memory_space=pl.ANY)
     dma = pltpu.SemaphoreType.DMA
     prefill_out, decode_out = pl.pallas_call(
         functools.partial(kernel, half, tps),
         out_shape=(
             jax.ShapeDtypeStruct((1, 2, rows, 1024 * tps), jnp.bfloat16),
-            jax.ShapeDtypeStruct((16, 1024), jnp.bfloat16),
+            jax.ShapeDtypeStruct((8, 2, 1024), jnp.bfloat16),
         ),
         in_specs=[anywhere] * 8,
-        out_specs=(anywhere, vmem),
+        out_specs=(anywhere, anywhere),
         scratch_shapes=[
             pltpu.SMEM(block_order.shape, jnp.int32),
             pltpu.SMEM(hist_len.shape, jnp.int32),
@@ -439,6 +439,8 @@
             dma((2, tps)),
             dma(()),
             pltpu.SemaphoreType.REGULAR((3,)),
+            pltpu.VMEM((8, 2, 1024), jnp.bfloat16),
+            dma(()),
         ],
         compiler_params=pltpu.CompilerParams(
             collective_id=0, has_side_effects=True, vmem_limit_bytes=63_400_000
@@ -464,9 +466,8 @@
         scratch_shapes=[
             pltpu.VMEM(prefill_out.shape[1:], jnp.bfloat16),
             pltpu.VMEM(decode_out.shape, jnp.bfloat16),
-            pltpu.VMEM(decode_query.shape[1:], jnp.bfloat16),
-            dma((3,)),
-            dma((3,)),
+            dma((5,)),
+            dma((5,)),
         ],
     )(prefill_out, decode_out)
 

time: 58.5 us -> 57.3 us (0.979)
  Pallas kernels: 57.5 us -> 56.3 us
    pallas_call x1, Pallas kernels: 55.7 us -> 54.5 us  [per_device(): pl.pallas_call(functools.partial(kernel, half, tps), out_shape=(jax.Shape...]
where the time goes in v4:
time: 57.3 us; the launch traced here: 57.1 us
  Pallas kernels  56.3 us (98%)
  between operations  0.8 us (1%)
    pallas_call x1, Pallas kernels, per_device(): pl.pallas_call(functools.partial(kernel, half, tps), out_shape=(jax.Shape...  54.5 us
    pallas_call x1, Pallas kernels, per_device(): pl.pallas_call(finish, out_shape=(jax.ShapeDtypeStruct(prefill_out.shape,...  1.86 us

profile of v4, /device:TPU:6, one launch (start us, length us, event | category | flops | bytes accessed | tf_op | source)
XLA Modules:
  0.0 57.1 jit_solution(10123430297727989302)
XLA Ops:
  0.6 54.5 %shard_map.95 = (bf16[1,2,16,8192]{3,2,1,0:T(8,128)(2,1)}, bf16[8,2,1024]{2,1,0:T(2,128)(2,1)}) custom-call(s32[1,2,32]{2,1,0:T(2,128)} %order_in.1, s32[1,8]{1,0:T(1,128)} %hist_len_in.1, s32[1,8]{1,0:T(1,128)} %row_prompt_in.1, bf16[1,2,128,1024]{3,2,1,0:T(8,128)(2,1)} %pq.1, bf16[1,2,2,128,128]{4,3,2,1,0:T(8,128)(2,1)} %pkv_in.1, ...), custom_call_target="tpu_custom_call" | custom-call | tf_op jit(solution)/shard_map/pallas_call | solution.py:398
  55.1 1.9 %shard_map.96 = (bf16[1,2,16,8192]{3,2,1,0:T(8,128)(2,1)}, bf16[1,8,2,1024]{3,2,1,0:T(2,128)(2,1)}) custom-call(bf16[1,2,16,8192]{3,2,1,0:T(8,128)(2,1)} %get-tuple-element.4.prefill, bf16[8,2,1024]{2,1,0:T(2,128)(2,1)} %get-tuple-element.5.decode), custom_call_target="tpu_custom_call" | custom-call | tf_op jit(solution)/shard_map/pallas_call | solution.py:458

commit v5 on v4

--- a/solution.py
+++ b/solution.py
@@ -266,8 +266,8 @@
             if after:
                 after(tiles[i])
 
-    def own(tiles):
-        attend(tiles, 0, (0, 1), [(z, yh), (z, 1 - yh)], first=True)
+    def own(tiles, between=()):
+        attend(tiles, 0, (0, 1), [(z, yh), (z, 1 - yh)], first=True, between=between)
 
     def step(k, tiles, between=()):
         attend(tiles, k, (0, 1, 2, 3), [(z - k, yh), (z - k, 1 - yh), (z + k, yh), (z + k, 1 - yh)], between=between)
@@ -281,15 +281,15 @@
         copy.wait_recv()
     for copy in d_copies:
         copy.wait_recv()
-    own([0, 1, 2, 3, 8])
     def at(k, places, last=0):
         return [(i, (k, b, h, last)) for i, (b, h) in zip(places, [(0, 0), (1, 0), (0, 1), (1, 1)])]
 
     early, late = [0, 1, 2, 3, 8], [4, 5, 6, 7]
     everything = [8, 4, 5, 6, 7, 0, 1, 2, 3]
-    step(1, early, at(2, (1, 2, 3, 4)))
+    own(early, at(2, (3, 4)))
+    step(1, early, [(0, (2, 0, 1)), (1, (2, 1, 1))] + at(3, (3, 4)))
     greet(1)
-    step(2, early, at(3, (1, 2, 3, 4)))
+    step(2, early, [(0, (3, 0, 1)), (1, (3, 1, 1))])
     q_copy.wait_recv()
     own(late)
     step(1, late, at(4, (1, 3)))

time: 57.3 us -> 57.7 us (level)
  no operation moved by 1% of the time
where the time goes in v5:
time: 57.7 us; the launch traced here: 57.3 us
  Pallas kernels  56.5 us (98%)
  between operations  0.8 us (1%)
    pallas_call x1, Pallas kernels, per_device(): pl.pallas_call(functools.partial(kernel, half, tps), out_shape=(jax.Shape...  54.6 us
    pallas_call x1, Pallas kernels, per_device(): pl.pallas_call(finish, out_shape=(jax.ShapeDtypeStruct(prefill_out.shape,...  1.86 us

profile of v5, /device:TPU:6, one launch (start us, length us, event | category | flops | bytes accessed | tf_op | source)
XLA Modules:
  0.0 57.3 jit_solution(12672292817842235470)
XLA Ops:
  0.6 54.6 %shard_map.95 = (bf16[1,2,16,8192]{3,2,1,0:T(8,128)(2,1)}, bf16[8,2,1024]{2,1,0:T(2,128)(2,1)}) custom-call(s32[1,2,32]{2,1,0:T(2,128)} %order_in.1, s32[1,8]{1,0:T(1,128)} %hist_len_in.1, s32[1,8]{1,0:T(1,128)} %row_prompt_in.1, bf16[1,2,128,1024]{3,2,1,0:T(8,128)(2,1)} %pq.1, bf16[1,2,2,128,128]{4,3,2,1,0:T(8,128)(2,1)} %pkv_in.1, ...), custom_call_target="tpu_custom_call" | custom-call | tf_op jit(solution)/shard_map/pallas_call | solution.py:398
  55.3 1.9 %shard_map.96 = (bf16[1,2,16,8192]{3,2,1,0:T(8,128)(2,1)}, bf16[1,8,2,1024]{3,2,1,0:T(2,128)(2,1)}) custom-call(bf16[1,2,16,8192]{3,2,1,0:T(8,128)(2,1)} %get-tuple-element.4.prefill, bf16[8,2,1024]{2,1,0:T(2,128)(2,1)} %get-tuple-element.5.decode), custom_call_target="tpu_custom_call" | custom-call | tf_op jit(solution)/shard_map/pallas_call | solution.py:458
